TPU v7x, 32 devices: a whole 2x2x4 slice. The times are simulated.
32 devices in a mesh: ctx: 8 (over z, y), wt: 4 (over x, core).
Axes of the slice: x: 2, y: 2, z: 4, core: 2. Of those that a mesh axis runs over, the one named last changes fastest.
Arguments:
- block_in: bfloat16 [4096, 1024], P('ctx'), may hold values from -6 to 6
- doc_ids: int32 [4096], replicated, may hold values from 0 to 3, as said below
- block_of: int32 [16], replicated, may hold values from 0 to 15, as said below
- w_query: bfloat16 [1024, 1024], P(None, 'wt'), may hold values from -0.1875 to 0.1875
- w_key: bfloat16 [1024, 512], P(None, 'wt'), may hold values from -0.1875 to 0.1875
- w_value: bfloat16 [1024, 512], P(None, 'wt'), may hold values from -0.1875 to 0.1875
- w_out: bfloat16 [1024, 1024], P('wt'), may hold values from -1.5 to 1.5
- w_gate: bfloat16 [1024, 4608], P(None, 'wt'), may hold values from -0.1875 to 0.1875
- w_up: bfloat16 [1024, 4608], P(None, 'wt'), may hold values from -0.1875 to 0.1875
- w_down: bfloat16 [4608, 1024], P('wt'), may hold values from -0.09375 to 0.09375
- attn_gain: float32 [1024], replicated, may hold values from 0.5 to 1.5
- ffn_gain: float32 [1024], replicated, may hold values from 0.5 to 1.5
- query_gain: float32 [64], replicated, may hold values from 1 to 2
- key_gain: float32 [64], replicated, may hold values from 0.1 to 1.9
- cotangent: bfloat16 [4096, 1024], P('ctx'), may hold values from -8 to 8
Outputs:
- block_out: bfloat16 [4096, 1024], P('ctx')
- input_grad: float32 [4096, 1024], P('ctx')
- grad_query: float32 [1024, 1024], P('ctx', 'wt')
- grad_key: float32 [1024, 512], P('ctx', 'wt')
- grad_value: float32 [1024, 512], P('ctx', 'wt')
- grad_out_proj: float32 [1024, 1024], P('wt', 'ctx')
- grad_gate: float32 [1024, 4608], P('ctx', 'wt')
- grad_up: float32 [1024, 4608], P('ctx', 'wt')
- grad_down: float32 [4608, 1024], P('wt', 'ctx')
- grad_attn_gain: float32 [1024], P('ctx')
- grad_ffn_gain: float32 [1024], P('ctx')
- grad_query_gain: float32 [64], P('ctx')
- grad_key_gain: float32 [64], P('ctx')
Inputs may be any that keep to these rules, and one draw needn't show every extreme that they name: doc_ids never falls along the text order, is 0 at the first token and 3 at the last, and document 0 holds at least the first 2048 tokens. block_of is a permutation of 0 to 15 whose entries 2c and 2c + 1 sum to 15 for every c.
All inputs are finite; a program needn't handle non-finite values.
Results may differ from a plain program's by a relative error of at most 0.029.
Values may be sent and summed in bfloat16 or wider, within the bound.
No kernel may reach another device: no remote copies, remote signals or barrier semaphores. Data moves between devices by JAX's collectives and lax.ppermute only.
A program may use at most 128 MiB of HBM per device.

v0:
```python
import math

import jax
import jax.numpy as jnp
from jax import lax
from jax.sharding import PartitionSpec as P

EPS = 1e-05
THETA = 1000000.0
NEG = -1e30
SCALE = 0.125


def rms_norm(vector, gain):
    return vector * lax.rsqrt(jnp.mean(vector * vector, axis=-1, keepdims=True) + EPS) * gain


def norm_back(vector, gain, gradient):
    inverse = lax.rsqrt(jnp.mean(vector * vector, axis=-1, keepdims=True) + EPS)
    scaled = gradient * gain
    back = inverse * scaled - vector * inverse**3 * jnp.mean(
        scaled * vector, axis=-1, keepdims=True
    )
    return (back, gradient * vector * inverse)


def rope_tables(positions, width):
    half_width = width // 2
    freqs = THETA ** (-2.0 * jnp.arange(half_width, dtype=jnp.float32) / width)
    angle = positions.astype(jnp.float32)[:, None] * freqs[None, :]
    return (jnp.cos(angle)[:, None, :], jnp.sin(angle)[:, None, :])


def rotate(vector, cos_table, sin_table):
    half_width = vector.shape[-1] // 2
    lead_part = vector[..., :half_width]
    tail_part = vector[..., half_width:]
    return jnp.concatenate(
        [
            lead_part * cos_table - tail_part * sin_table,
            tail_part * cos_table + lead_part * sin_table,
        ],
        axis=-1,
    )


def matmul(left, right):
    return jnp.dot(left, right, preferred_element_type=jnp.float32)


def on_device(
    block_in,
    doc_ids,
    block_of,
    w_query,
    w_key,
    w_value,
    w_out,
    w_gate,
    w_up,
    w_down,
    attn_gain,
    ffn_gain,
    query_gain,
    key_gain,
    cotangent,
):
    tok_rows = block_in.shape[0]
    head_dim = query_gain.shape[0]
    heads_here = w_query.shape[1] // head_dim
    kv_here = w_key.shape[1] // head_dim
    kv_width = kv_here * head_dim
    groups = heads_here // kv_here
    total_rows = tok_rows * lax.axis_size("ctx")
    half_rows = tok_rows // 2
    key_pos = (
        block_of[:, None] * half_rows + jnp.arange(half_rows, dtype=jnp.int32)[None, :]
    ).reshape(total_rows)
    key_doc = jnp.take(doc_ids, key_pos)
    own_start = lax.axis_index("ctx") * tok_rows
    query_pos = lax.dynamic_slice_in_dim(key_pos, own_start, tok_rows)
    query_doc = lax.dynamic_slice_in_dim(key_doc, own_start, tok_rows)
    cos_table, sin_table = rope_tables(query_pos, head_dim)
    inputs = block_in.astype(jnp.float32)
    normed_one = rms_norm(inputs, attn_gain).astype(jnp.bfloat16)
    query_raw = matmul(normed_one, w_query).reshape(tok_rows, heads_here, head_dim)
    key_raw = matmul(normed_one, w_key).reshape(tok_rows, kv_here, head_dim)
    value_low = matmul(normed_one, w_value).astype(jnp.bfloat16)
    query_low = rotate(rms_norm(query_raw, query_gain), cos_table, sin_table).astype(jnp.bfloat16)
    key_low = (
        rotate(rms_norm(key_raw, key_gain), cos_table, sin_table)
        .astype(jnp.bfloat16)
        .reshape(tok_rows, kv_width)
    )
    query_heads = query_low.reshape(tok_rows, kv_here, groups, head_dim).transpose(1, 2, 0, 3)

    def tile_visible(offset, row_count):
        tile_pos = lax.dynamic_slice_in_dim(key_pos, offset, row_count)
        tile_doc = lax.dynamic_slice_in_dim(key_doc, offset, row_count)
        first_pos = jnp.min(tile_pos)
        doc_low = jnp.min(tile_doc)
        doc_high = jnp.max(tile_doc)
        return jnp.any((query_pos >= first_pos) & (query_doc >= doc_low) & (query_doc <= doc_high))

    def tile_scores(key_tile, offset, row_count):
        key_view = key_tile.reshape(row_count, kv_here, head_dim)
        scores = (
            jnp.einsum("kgqd,tkd->kgqt", query_heads, key_view, preferred_element_type=jnp.float32)
            * SCALE
        )
        tile_pos = lax.dynamic_slice_in_dim(key_pos, offset, row_count)
        tile_doc = lax.dynamic_slice_in_dim(key_doc, offset, row_count)
        allowed = (query_doc[:, None] == tile_doc[None, :]) & (
            tile_pos[None, :] <= query_pos[:, None]
        )
        return jnp.where(allowed, scores, NEG)

    initial = (
        jnp.full((kv_here, groups, tok_rows), NEG, jnp.float32),
        jnp.zeros((kv_here, groups, tok_rows), jnp.float32),
        jnp.zeros((kv_here, groups, tok_rows, head_dim), jnp.float32),
    )
    keys_all, values_all = (
        lax.all_gather(key_low, "ctx", axis=0, tiled=True),
        lax.all_gather(value_low, "ctx", axis=0, tiled=True),
    )
    carried = initial
    row_count = keys_all.shape[0]
    tile_rows = math.gcd(row_count, half_rows)

    def attend_one_tile(state, tile_index):
        tile_begin = tile_index * tile_rows
        key_tile = lax.dynamic_slice_in_dim(keys_all, tile_begin, tile_rows, 0)
        value_tile = lax.dynamic_slice_in_dim(values_all, tile_begin, tile_rows, 0).reshape(
            tile_rows, kv_here, head_dim
        )

        def attend_take_tile(old):
            row_best, row_total, summed = old
            scores = tile_scores(key_tile, 0 + tile_begin, tile_rows)
            new_best = jnp.maximum(row_best, jnp.max(scores, axis=-1))
            factor = jnp.exp(row_best - new_best)
            weights = jnp.exp(scores - new_best[..., None])
            new_total = row_total * factor + jnp.sum(weights, axis=-1)
            new_summed = summed * factor[..., None] + jnp.einsum(
                "kgqt,tkd->kgqd",
                weights.astype(jnp.bfloat16),
                value_tile,
                preferred_element_type=jnp.float32,
            )
            return (new_best, new_total, new_summed)

        def attend_skip_tile(old):
            return old

        return (
            lax.cond(
                tile_visible(0 + tile_begin, tile_rows), attend_take_tile, attend_skip_tile, state
            ),
            None,
        )

    carried, _ = lax.scan(
        attend_one_tile, carried, jnp.arange(row_count // tile_rows, dtype=jnp.int32)
    )
    row_best, row_total, summed = carried
    attn_out = summed / row_total[..., None]
    log_total = row_best + jnp.log(row_total)
    out_low = (
        attn_out.transpose(2, 0, 1, 3).reshape(tok_rows, heads_here * head_dim).astype(jnp.bfloat16)
    )
    attn_sum = lax.psum(matmul(out_low, w_out).astype(jnp.bfloat16), "wt").astype(jnp.float32)
    middle = inputs + attn_sum
    normed_two = rms_norm(middle, ffn_gain).astype(jnp.bfloat16)
    gate_proj = matmul(normed_two, w_gate)
    up_proj = matmul(normed_two, w_up)
    sigmoid_gate = jax.nn.sigmoid(gate_proj)
    silu_gate = gate_proj * sigmoid_gate
    hidden = (silu_gate * up_proj).astype(jnp.bfloat16)
    ffn_sum = lax.psum(matmul(hidden, w_down).astype(jnp.bfloat16), "wt").astype(jnp.float32)
    block_out = (middle + ffn_sum).astype(jnp.bfloat16)
    grad_down = matmul(hidden.T, cotangent)
    grad_hidden = matmul(cotangent, w_down.T)
    grad_gate = (
        grad_hidden * up_proj * sigmoid_gate * (1.0 + gate_proj * (1.0 - sigmoid_gate))
    ).astype(jnp.bfloat16)
    grad_upper = (grad_hidden * silu_gate).astype(jnp.bfloat16)
    grad_w_gate = matmul(normed_two.T, grad_gate)
    grad_w_up = matmul(normed_two.T, grad_upper)
    normed_two_grad = lax.psum(
        (matmul(grad_gate, w_gate.T) + matmul(grad_upper, w_up.T)).astype(jnp.bfloat16), "wt"
    ).astype(jnp.float32)
    middle_back, ffn_gain_terms = norm_back(middle, ffn_gain, normed_two_grad)
    grad_middle = cotangent.astype(jnp.float32) + middle_back
    grad_middle_low = grad_middle.astype(jnp.bfloat16)
    grad_w_out = matmul(out_low.T, grad_middle_low)
    grad_attended = matmul(grad_middle_low, w_out.T).astype(jnp.bfloat16)
    grad_heads = grad_attended.reshape(tok_rows, kv_here, groups, head_dim).transpose(1, 2, 0, 3)
    row_delta = jnp.sum(grad_heads.astype(jnp.float32) * attn_out, axis=-1)

    def back_tile(key_tile, value_tile, offset, row_count):
        scores = tile_scores(key_tile, offset, row_count)
        probabilities = jnp.exp(scores - log_total[..., None])
        key_view = key_tile.reshape(row_count, kv_here, head_dim)
        value_view = value_tile.reshape(row_count, kv_here, head_dim)
        grad_value_tile = jnp.einsum(
            "kgqt,kgqd->tkd",
            probabilities.astype(jnp.bfloat16),
            grad_heads,
            preferred_element_type=jnp.float32,
        )
        grad_probs = jnp.einsum(
            "kgqd,tkd->kgqt", grad_heads, value_view, preferred_element_type=jnp.float32
        )
        grad_scores = (probabilities * (grad_probs - row_delta[..., None])).astype(jnp.bfloat16)
        grad_query_tile = (
            jnp.einsum("kgqt,tkd->kgqd", grad_scores, key_view, preferred_element_type=jnp.float32)
            * SCALE
        )
        grad_key_tile = (
            jnp.einsum(
                "kgqt,kgqd->tkd", grad_scores, query_heads, preferred_element_type=jnp.float32
            )
            * SCALE
        )
        return (
            grad_query_tile,
            grad_key_tile.reshape(row_count, kv_width),
            grad_value_tile.reshape(row_count, kv_width),
        )

    back_tile_rows = math.gcd(total_rows, half_rows)

    def back_one_tile(grad_acc, tile_index):
        tile_begin = tile_index * back_tile_rows
        key_tile = lax.dynamic_slice_in_dim(keys_all, tile_begin, back_tile_rows, 0)
        value_tile = lax.dynamic_slice_in_dim(values_all, tile_begin, back_tile_rows, 0)

        def back_take_tile(unused):
            return back_tile(key_tile, value_tile, 0 + tile_begin, back_tile_rows)

        def back_skip_tile(unused):
            return (
                jnp.zeros((kv_here, groups, tok_rows, head_dim), jnp.float32),
                jnp.zeros((back_tile_rows, kv_width), jnp.float32),
                jnp.zeros((back_tile_rows, kv_width), jnp.float32),
            )

        query_part, key_part, value_part = lax.cond(
            tile_visible(0 + tile_begin, back_tile_rows), back_take_tile, back_skip_tile, 0
        )
        return (grad_acc + query_part, (key_part, value_part))

    zeros_query = jnp.zeros((kv_here, groups, tok_rows, head_dim), jnp.float32)
    grad_query_heads, (key_tiles, value_tiles) = lax.scan(
        back_one_tile, zeros_query, jnp.arange(total_rows // back_tile_rows, dtype=jnp.int32)
    )
    key_grad, value_grad = (
        lax.psum_scatter(
            key_tiles.reshape(total_rows, kv_width).astype(jnp.bfloat16),
            "ctx",
            scatter_dimension=0,
            tiled=True,
        ).astype(jnp.float32),
        lax.psum_scatter(
            value_tiles.reshape(total_rows, kv_width).astype(jnp.bfloat16),
            "ctx",
            scatter_dimension=0,
            tiled=True,
        ).astype(jnp.float32),
    )
    query_back = rotate(
        grad_query_heads.transpose(2, 0, 1, 3).reshape(tok_rows, heads_here, head_dim),
        cos_table,
        -sin_table,
    )
    query_raw_grad, query_gain_terms = norm_back(query_raw, query_gain, query_back)
    query_raw_low = query_raw_grad.reshape(tok_rows, heads_here * head_dim).astype(jnp.bfloat16)
    key_back = rotate(key_grad.reshape(tok_rows, kv_here, head_dim), cos_table, -sin_table)
    key_raw_grad, key_gain_terms = norm_back(key_raw, key_gain, key_back)
    key_raw_low = key_raw_grad.reshape(tok_rows, kv_width).astype(jnp.bfloat16)
    value_raw_low = value_grad.astype(jnp.bfloat16)
    grad_w_query = matmul(normed_one.T, query_raw_low)
    grad_w_key = matmul(normed_one.T, key_raw_low)
    grad_w_value = matmul(normed_one.T, value_raw_low)
    normed_one_part = (
        matmul(query_raw_low, w_query.T)
        + matmul(key_raw_low, w_key.T)
        + matmul(value_raw_low, w_value.T)
    )
    normed_one_grad, query_gain_grad, key_gain_grad = (
        lax.psum(normed_one_part.astype(jnp.bfloat16), "wt").astype(jnp.float32),
        lax.psum(jnp.sum(query_gain_terms, axis=(0, 1)).astype(jnp.bfloat16), "wt").astype(
            jnp.float32
        ),
        lax.psum(jnp.sum(key_gain_terms, axis=(0, 1)).astype(jnp.bfloat16), "wt").astype(
            jnp.float32
        ),
    )
    input_back, attn_gain_terms = norm_back(inputs, attn_gain, normed_one_grad)
    input_grad = grad_middle + input_back
    outs_in = (
        lax.psum_scatter(
            grad_w_query.astype(jnp.bfloat16), "ctx", scatter_dimension=0, tiled=True
        ).astype(jnp.float32),
        lax.psum_scatter(
            grad_w_key.astype(jnp.bfloat16), "ctx", scatter_dimension=0, tiled=True
        ).astype(jnp.float32),
        lax.psum_scatter(
            grad_w_value.astype(jnp.bfloat16), "ctx", scatter_dimension=0, tiled=True
        ).astype(jnp.float32),
        lax.psum_scatter(
            grad_w_gate.astype(jnp.bfloat16), "ctx", scatter_dimension=0, tiled=True
        ).astype(jnp.float32),
        lax.psum_scatter(
            grad_w_up.astype(jnp.bfloat16), "ctx", scatter_dimension=0, tiled=True
        ).astype(jnp.float32),
        lax.psum_scatter(
            jnp.sum(attn_gain_terms, axis=0).astype(jnp.bfloat16),
            "ctx",
            scatter_dimension=0,
            tiled=True,
        ).astype(jnp.float32),
        lax.psum_scatter(
            jnp.sum(ffn_gain_terms, axis=0).astype(jnp.bfloat16),
            "ctx",
            scatter_dimension=0,
            tiled=True,
        ).astype(jnp.float32),
        lax.psum_scatter(
            query_gain_grad.astype(jnp.bfloat16), "ctx", scatter_dimension=0, tiled=True
        ).astype(jnp.float32),
        lax.psum_scatter(
            key_gain_grad.astype(jnp.bfloat16), "ctx", scatter_dimension=0, tiled=True
        ).astype(jnp.float32),
    )
    grad_out_proj, grad_down_proj = (
        lax.psum_scatter(
            grad_w_out.astype(jnp.bfloat16), "ctx", scatter_dimension=1, tiled=True
        ).astype(jnp.float32),
        lax.psum_scatter(
            grad_down.astype(jnp.bfloat16), "ctx", scatter_dimension=1, tiled=True
        ).astype(jnp.float32),
    )
    return (
        block_out,
        input_grad,
        outs_in[0],
        outs_in[1],
        outs_in[2],
        grad_out_proj,
        outs_in[3],
        outs_in[4],
        grad_down_proj,
        outs_in[5],
        outs_in[6],
        outs_in[7],
        outs_in[8],
    )


def solution(mesh):
    in_specs = (
        P("ctx", None),
        P(),
        P(),
        P(None, "wt"),
        P(None, "wt"),
        P(None, "wt"),
        P("wt", None),
        P(None, "wt"),
        P(None, "wt"),
        P("wt", None),
        P(),
        P(),
        P(),
        P(),
        P("ctx", None),
    )
    out_specs = (
        P("ctx", None),
        P("ctx", None),
        P("ctx", "wt"),
        P("ctx", "wt"),
        P("ctx", "wt"),
        P("wt", "ctx"),
        P("ctx", "wt"),
        P("ctx", "wt"),
        P("wt", "ctx"),
        P("ctx"),
        P("ctx"),
        P("ctx"),
        P("ctx"),
    )
    return jax.shard_map(
        on_device, mesh=mesh, in_specs=in_specs, out_specs=out_specs, check_vma=False
    )
```

profile of v0, /device:TPU:0, one launch (start us, length us, event | category | flops | bytes accessed | tf_op | source)
XLA Modules:
  0.0 1275.5 jit_solution(9848711325418071915)
XLA Ops:
  18.2 23.0 %gather_fusion = s32[4096]{0:T(1024)S(1)} fusion(s32[4096]{0:T(1024)S(1)} %copy-done.1, s32[4096]{0:T(1024)S(1)} %broadcast_clamp_fusion), kind=kCustom, calls=%fused_computation | custom fusion | bytes 49152 | tf_op jit(solution)/shard_map/jit(_take)/gather | solution.py:79
  46.8 8.3 all-gather.5.cloned.1.call-done
  57.3 38.6 %all-gather.3.cloned.1.call-done = bf16[4096,128]{0,1:T(8,128)(2,1)} async-done(((bf16[512,128]{0,1:T(8,128)(2,1)}), bf16[4096,128]{0,1:T(8,128)(2,1)}) %all-gather.3.cloned.1.call-update) | async-done | bytes 1048592 | tf_op jit(solution)/shard_map/all_gather | solution.py:124
  96.8 149.2 %while.29 = (s32[]{:T(128)}, f32[2,2,512]{2,1,0:T(2,128)S(1)}, f32[2,2,512]{2,1,0:T(2,128)S(1)}, f32[2,2,512,64]{2,3,1,0:T(8,128)}, s32[16]{0:T(128)S(1)}, /*ind...) while((s32[]{:T(128)}, f32[2,2,512]{2,1,0:T(2,128)S(1)}, ...), condition=%wide.region_12.13_spmd, body=%wide.region_3.12_spmd.sunk | while | flops 138551040 | bytes 12599791 | solution.py:163
  102.7 6.1 conditional.5
  114.7 6.1 conditional.5
  132.6 6.1 conditional.5
  144.6 6.1 conditional.5
  162.5 6.1 conditional.5
  198.3 6.1 conditional.5
  250.6 52.0 %all-reduce.11.cloned.1.call-done = bf16[512,1024]{1,0:T(8,128)(2,1)} async-done(((bf16[512,1024]{1,0:T(8,128)(2,1)}), bf16[512,1024]{1,0:T(8,128)(2,1)}) %all-reduce.11.cloned.1.call-update) | async-done | bytes 1048592 | tf_op jit(solution)/shard_map/psum | solution.py:172
  317.7 35.9 %all-reduce.13.cloned.1.call-done = bf16[512,1024]{1,0:T(8,128)(2,1)} async-done(((bf16[512,1024]{1,0:T(8,128)(2,1)}), bf16[512,1024]{1,0:T(8,128)(2,1)}) %all-reduce.13.cloned.1.call-update) | async-done | bytes 1048592 | tf_op jit(solution)/shard_map/psum | solution.py:190
  359.8 233.9 %while.30 = (s32[]{:T(128)}, f32[2,2,512,64]{2,3,1,0:T(8,128)}, bf16[16,256,128]{2,1,0:T(8,128)(2,1)}, bf16[16,256,128]{2,1,0:T(8,128)(2,1)}, s32[16]{0:T(128)},...) while((s32[]{:T(128)}, f32[2,2,512,64]{2,3,1,0:T(8,128)}, ...), condition=%wide.region_26.27_spmd.clone, body=%wide.region_19.26_spmd.clone.sunk | while | flops 340070144 | bytes 13993401 | solution.py:255
  606.1 67.1 %reduce-scatter.14.cloned.1.call-done = bf16[512,128]{1,0:T(8,128)(2,1)} async-done(((bf16[4096,128]{1,0:T(8,128)(2,1)}), bf16[512,128]{1,0:T(8,128)(2,1)}) %reduce-scatter.14.cloned.1.call-update) | async-done | bytes 131088 | tf_op jit(solution)/shard_map/reduce_scatter | solution.py:259
  682.7 56.4 %reduce-scatter.16.cloned.1.call-done = bf16[512,128]{1,0:T(8,128)(2,1)} async-done(((bf16[4096,128]{1,0:T(8,128)(2,1)}), bf16[512,128]{1,0:T(8,128)(2,1)}) %reduce-scatter.16.cloned.1.call-update) | async-done | bytes 131088 | tf_op jit(solution)/shard_map/reduce_scatter | solution.py:265
  766.6 36.9 %reduce-scatter.28.cloned.1.call-done = bf16[128,256]{1,0:T(8,128)(2,1)} async-done(((bf16[1024,256]{1,0:T(8,128)(2,1)}), bf16[128,256]{1,0:T(8,128)(2,1)}) %reduce-scatter.28.cloned.1.call-update) | async-done | bytes 65552
  805.1 63.6 %reduce-scatter.18.cloned.1.call-done = bf16[128,256]{1,0:T(8,128)(2,1)} async-done(((bf16[1024,256]{1,0:T(8,128)(2,1)}), bf16[128,256]{1,0:T(8,128)(2,1)}) %reduce-scatter.18.cloned.1.call-update) | async-done | bytes 65552 | tf_op jit(solution)/shard_map/reduce_scatter | solution.py:303
  870.3 62.5 %reduce-scatter.20.cloned.1.call-done = bf16[128,128]{1,0:T(8,128)(2,1)} async-done(((bf16[1024,128]{1,0:T(8,128)(2,1)}), bf16[128,128]{1,0:T(8,128)(2,1)}) %reduce-scatter.20.cloned.1.call-update) | async-done | bytes 32784 | tf_op jit(solution)/shard_map/reduce_scatter | solution.py:306
  934.2 52.1 %all-reduce.15.cloned.1.call-done = (bf16[512,1024]{1,0:T(8,128)(2,1)}, bf16[512,1024]{1,0:T(8,128)(2,1)}) async-done(((bf16[512,1024]{1,0:T(8,128)(2,1)}, bf16[512,1024]{1,0:T(8,128)(2,1)}), (bf16[512,1024]{1,0:T(8,128)(2,1)}, bf16[512,1024]{1,0:T(8,128)(2,1)})) %all-reduce.15.cloned.1.call-update) | async-done | bytes 2097168 | tf_op jit(solution)/shard_map/psum | solution.py:180
  988.4 21.7 %all-reduce.4 = (bf16[1024]{0:T(1024)(128)(2,1)S(1)}, bf16[1024]{0:T(1024)(128)(2,1)S(1)}, bf16[64]{0:T(256)(128)(2,1)S(1)}, bf16[64]{0:T(256)(128)(2,1)S(1)}) all-reduce(bf16[1024]{0:T(1024)(128)(2,1)S(1)} %get-tuple-element.555, bf16[1024]{0:T(1024)(128)(2,1)S(1)} %copy-done.43, ...), channel_id=11, replica_groups=mesh['ctx'=8,'wt'=4] {'ctx'}, use_global_device_ids=true, to_apply=%region_41.42.clone | all-reduce | flops 2176 | bytes 8704
  1010.3 41.7 %reduce-scatter.22.cloned.1.call-done = bf16[128,128]{1,0:T(8,128)(2,1)} async-done(((bf16[1024,128]{1,0:T(8,128)(2,1)}), bf16[128,128]{1,0:T(8,128)(2,1)}) %reduce-scatter.22.cloned.1.call-update) | async-done | bytes 32784 | tf_op jit(solution)/shard_map/reduce_scatter | solution.py:309
  1065.9 57.9 %reduce-scatter.30.cloned.1.call-done = bf16[128,1152]{1,0:T(8,128)(2,1)} async-done(((bf16[1024,1152]{1,0:T(8,128)(2,1)}), bf16[128,1152]{1,0:T(8,128)(2,1)}) %reduce-scatter.30.cloned.1.call-update) | async-done | bytes 294928
  1125.8 69.7 %reduce-scatter.24.cloned.1.call-done = bf16[128,1152]{1,0:T(8,128)(2,1)} async-done(((bf16[1024,1152]{1,0:T(8,128)(2,1)}), bf16[128,1152]{1,0:T(8,128)(2,1)}) %reduce-scatter.24.cloned.1.call-update) | async-done | bytes 294928 | tf_op jit(solution)/shard_map/reduce_scatter | solution.py:312
  1197.4 69.8 %reduce-scatter.26.cloned.1.call-done = bf16[128,1152]{1,0:T(8,128)(2,1)} async-done(((bf16[1024,1152]{1,0:T(8,128)(2,1)}), bf16[128,1152]{1,0:T(8,128)(2,1)}) %reduce-scatter.26.cloned.1.call-update) | async-done | bytes 294928 | tf_op jit(solution)/shard_map/reduce_scatter | solution.py:315
  (663 shorter events, 531.4 us)
Async XLA Ops:
  7.2 302.4 %copy-start = (bf16[1152,1024]{1,0:T(8,128)(2,1)S(1)}, bf16[1152,1024]{1,0:T(8,128)(2,1)}, u32[]{:S(2)}) copy-start(bf16[1152,1024]{1,0:T(8,128)(2,1)} %param.32) | copy-start | bytes 7077892
  7.2 47.8 %all-gather.5.cloned.1.call-start = ((), (), s32[]{:S(2)}) async-start(), calls=%async_computation.10 | async-start | bytes 1179648 | tf_op jit(solution)/shard_map/all_gather | solution.py:125
  9.5 33.8 %copy-start.37 = (f32[512]{0:T(512)}, f32[512]{0:T(512)S(1)}, u32[]{:S(2)}) copy-start(f32[512]{0:T(512)S(1)} %get-tuple-element.660) | copy-start | bytes 6148
  12.0 84.0 %all-gather.3.cloned.1.call-start = ((), (), s32[]{:S(2)}) async-start(), calls=%async_computation.9 | async-start | bytes 1179648 | tf_op jit(solution)/shard_map/all_gather | solution.py:124
  16.7 29.2 %copy-start.20 = (f32[512,32]{0,1:T(8,128)}, f32[512,32]{0,1:T(8,128)S(1)}, u32[]{:S(2)}) copy-start(f32[512,32]{0,1:T(8,128)S(1)} %get-tuple-element.658) | copy-start | bytes 196612
  18.0 284.5 %all-reduce.11.cloned.1.call-start = ((), (), s32[]{:S(2)}) async-start(), calls=%async_computation.11 | async-start | bytes 2097152 | tf_op jit(solution)/shard_map/psum | solution.py:172
  45.7 11.6 copy-start.31
  247.8 56.5 %copy-start.35 = (f32[1024]{0:T(1024)S(1)}, f32[1024]{0:T(1024)}, u32[]{:S(2)}) copy-start(f32[1024]{0:T(1024)} %param.34) | copy-start | bytes 12292
  250.3 103.3 %all-reduce.13.cloned.1.call-start = ((), (), s32[]{:S(2)}) async-start(), calls=%async_computation.12 | async-start | bytes 2097152 | tf_op jit(solution)/shard_map/psum | solution.py:190
  317.0 356.1 %reduce-scatter.14.cloned.1.call-start = ((), (), s32[]{:S(2)}) async-start(), calls=%async_computation.13 | async-start | bytes 1179648 | tf_op jit(solution)/shard_map/reduce_scatter | solution.py:259
  593.8 145.4 %reduce-scatter.16.cloned.1.call-start = ((), (), s32[]{:S(2)}) async-start(), calls=%async_computation.14 | async-start | bytes 1179648 | tf_op jit(solution)/shard_map/reduce_scatter | solution.py:265
  594.3 209.1 %reduce-scatter.28.cloned.1.call-start = ((), (), s32[]{:S(2)}) async-start(), calls=%async_computation.20 | async-start | bytes 589824
  598.4 270.3 %reduce-scatter.18.cloned.1.call-start = ((), (), s32[]{:S(2)}) async-start(), calls=%async_computation.15 | async-start | bytes 589824 | tf_op jit(solution)/shard_map/reduce_scatter | solution.py:303
  604.5 72.4 %copy-start.34 = (f32[512,2]{0,1:T(2,128)S(1)}, f32[512,2]{0,1:T(2,128)}, u32[]{:S(2)}) copy-start(f32[512,2]{0,1:T(2,128)} %copy-done.33) | copy-start | bytes 12292
  604.5 72.4 %copy-start.41 = (f32[512,2]{0,1:T(2,128)S(1)}, f32[512,2]{0,1:T(2,128)}, u32[]{:S(2)}) copy-start(f32[512,2]{0,1:T(2,128)} %get-tuple-element.654) | copy-start | bytes 12292
  606.0 326.8 %reduce-scatter.20.cloned.1.call-start = ((), (), s32[]{:S(2)}) async-start(), calls=%async_computation.16 | async-start | bytes 294912 | tf_op jit(solution)/shard_map/reduce_scatter | solution.py:306
  682.7 303.7 %all-reduce.15.cloned.1.call-start = ((), (), s32[]{:S(2)}) async-start(), calls=%async_computation.22 | async-start | bytes 4194304 | tf_op jit(solution)/shard_map/psum | solution.py:180
  743.5 308.5 %reduce-scatter.22.cloned.1.call-start = ((), (), s32[]{:S(2)}) async-start(), calls=%async_computation.17 | async-start | bytes 294912 | tf_op jit(solution)/shard_map/reduce_scatter | solution.py:309
  745.8 378.0 %reduce-scatter.30.cloned.1.call-start = ((), (), s32[]{:S(2)}) async-start(), calls=%async_computation.21 | async-start | bytes 2654208
  754.6 440.9 %reduce-scatter.24.cloned.1.call-start = ((), (), s32[]{:S(2)}) async-start(), calls=%async_computation.18 | async-start | bytes 2654208 | tf_op jit(solution)/shard_map/reduce_scatter | solution.py:312
  759.3 507.9 %reduce-scatter.26.cloned.1.call-start = ((), (), s32[]{:S(2)}) async-start(), calls=%async_computation.19 | async-start | bytes 2654208 | tf_op jit(solution)/shard_map/reduce_scatter | solution.py:315
  764.0 106.3 %copy-start.49 = (f32[128]{0:T(128)S(1)}, f32[128]{0:T(128)}, u32[]{:S(2)}) copy-start(f32[128]{0:T(128)} %get-tuple-element.642) | copy-start | bytes 1540
  764.0 224.5 %copy-start.43 = (bf16[1024]{0:T(1024)(128)(2,1)S(1)}, bf16[1024]{0:T(1024)(128)(2,1)}, u32[]{:S(2)}) copy-start(bf16[1024]{0:T(1024)(128)(2,1)} %get-tuple-element.553) | copy-start | bytes 6148
  764.0 296.7 %copy-start.42 = (f32[512]{0:T(512)S(1)}, f32[512]{0:T(512)}, u32[]{:S(2)}) copy-start(f32[512]{0:T(512)} %get-tuple-element.659) | copy-start | bytes 6148
  (62 other events, 132.7 us)
Sparse Core Ops, SparseCore 0:
  12.1 42.8 all-gather.4
  57.7 38.2 all-gather.2
  250.5 52.0 all-reduce.10
  317.1 36.4 all-reduce.12
  593.9 79.2 reduce-scatter.13
  676.8 62.3 reduce-scatter.15
  742.5 60.9 reduce-scatter.27
  807.8 60.9 reduce-scatter.17
  872.6 60.1 reduce-scatter.19
  935.7 50.5 all-reduce.14
  990.6 61.3 reduce-scatter.21
  1055.7 67.9 reduce-scatter.29
  1127.7 67.8 reduce-scatter.23
  1199.3 67.8 reduce-scatter.25
where the time goes:
time: 1290 us; the launch traced here: 1280 us
  waiting for transfers between devices  713 us (55%)
  other arithmetic  203 us (16%)
  local copies, waits for them, and re-layouts  176 us (14%)
  matrix products  95.7 us (7%)
  loops' own time  42.7 us (3%)
  blocking collectives  27.3 us (2%)
  between operations  15.8 us (1%)
    unnamed x16, waiting for transfers between devices  95.5 us
    reduce_or x32, other arithmetic, tile_visible(): jnp.any((query_pos >= first_pos) & (query_doc >= doc_low) & (query_doc <=...  82.3 us
    reduce_scatter x1, waiting for transfers between devices, on_device(): lax.psum_scatter(grad_w_up.astype(jnp.bfloat16), 'ctx', scatter_dimension...  69.8 us
    reduce_scatter x1, waiting for transfers between devices, on_device(): lax.psum_scatter(grad_w_gate.astype(jnp.bfloat16), 'ctx', scatter_dimensi...  69.7 us
    reduce_scatter x1, waiting for transfers between devices, on_device(): lax.psum_scatter(key_tiles.reshape(total_rows, kv_width).astype(jnp.bfloa...  67.1 us
    reduce_scatter x1, waiting for transfers between devices, on_device(): lax.psum_scatter(grad_w_query.astype(jnp.bfloat16), 'ctx', scatter_dimens...  63.6 us
    reduce_scatter x1, waiting for transfers between devices, on_device(): lax.psum_scatter(grad_w_key.astype(jnp.bfloat16), 'ctx', scatter_dimensio...  62.5 us
    reduce_scatter x1, waiting for transfers between devices, on_device(): lax.psum_scatter(value_tiles.reshape(total_rows, kv_width).astype(jnp.bfl...  56.4 us
  transfers between devices with their start and end apart: 14, of which 14 were waited for; matrix products, arithmetic and copies ran while one was open for 8% of the time, Pallas kernels for 0%

commit v1 on v0

v1 whole, which is shorter than its diff:
```python
import functools

import jax
import jax.numpy as jnp
import numpy as np
from jax import lax
from jax.experimental import pallas as pl
from jax.experimental.pallas import tpu as pltpu
from jax.sharding import PartitionSpec as P

EPS = 1e-05
THETA = 1000000.0
NEG = -1e30
SCALE = 0.125
LANES = 128
DOCS = 4
VMEM_LIMIT = 60 * 1024 * 1024
F32 = jnp.float32
BF16 = jnp.bfloat16


def matmul(left, right):
    return jnp.dot(left, right, preferred_element_type=F32)


def contract(left, right, left_dim, right_dim):
    return lax.dot_general(
        left, right, (((left_dim,), (right_dim,)), ((), ())), preferred_element_type=F32
    )


def rms_norm(vector, gain):
    return vector * lax.rsqrt(jnp.mean(vector * vector, axis=-1, keepdims=True) + EPS) * gain


def norm_back(vector, gain, gradient):
    inverse = lax.rsqrt(jnp.mean(vector * vector, axis=-1, keepdims=True) + EPS)
    scaled = gradient * gain
    back = inverse * scaled - vector * inverse**3 * jnp.mean(
        scaled * vector, axis=-1, keepdims=True
    )
    return (back, gradient * vector * inverse)


def lane_index(shape):
    return lax.broadcasted_iota(jnp.int32, shape, len(shape) - 1)


def head_mean(values, head_dim):
    row_id = lax.broadcasted_iota(jnp.int32, (LANES, LANES), 0) // head_dim
    col_id = lax.broadcasted_iota(jnp.int32, (LANES, LANES), 1) // head_dim
    ones = (row_id == col_id).astype(BF16)
    high = values.astype(BF16)
    low = (values - high.astype(F32)).astype(BF16)
    return (matmul(high, ones) + matmul(low, ones)) * (1.0 / head_dim)


def swap_halves(values, head_dim):
    half = head_dim // 2
    lane = lane_index(values.shape)
    return jnp.where(
        lane % head_dim < half,
        pltpu.roll(values, LANES - half, 1),
        pltpu.roll(values, half, 1),
    )


def mix_heads(first, second, head_dim):
    lane = lane_index(first.shape)
    return (
        jnp.where(lane < head_dim, first, pltpu.roll(second, head_dim, 1)),
        jnp.where(lane < head_dim, pltpu.roll(first, head_dim, 1), second),
    )


def mix_low(first, second, head_dim):
    one, two = mix_heads(first.astype(F32), second.astype(F32), head_dim)
    return one.astype(BF16), two.astype(BF16)


def block_tables(base_cos, base_sin, step_cos, step_sin, head_dim):
    cos = base_cos * step_cos - base_sin * step_sin
    sin = base_sin * step_cos + base_cos * step_sin
    lane = lane_index(cos.shape)
    return cos, jnp.where(lane % head_dim < head_dim // 2, -sin, sin)


def head_norm_back(raw, gain, gradient, head_dim):
    inverse = lax.rsqrt(head_mean(raw * raw, head_dim) + EPS)
    scaled = gradient * gain
    back = inverse * scaled - raw * inverse**3 * head_mean(scaled * raw, head_dim)
    return back, jnp.sum(gradient * raw * inverse, axis=0, keepdims=True)


class Info:
    def __init__(self, ref, devices, half_rows):
        self.ref, self.devices, self.half_rows = ref, devices, half_rows
        self.ctx, self.core = ref[0], ref[1]

    def block(self, source, half):
        return self.ref[1 + DOCS + 2 * source + jnp.bitwise_xor(half, self.core)]

    def slot_source(self, slot):
        pairs = self.devices // 2
        same = slot < pairs
        column = jnp.where(same, self.ctx, jnp.bitwise_xor(self.ctx, 1))
        step = jnp.where(same, slot, slot - pairs)
        return lax.rem(column - 2 * step + self.devices, self.devices)

    def doc_start(self, position):
        start = jnp.zeros_like(position)
        for doc in range(1, DOCS):
            first = self.ref[1 + doc]
            start = jnp.where(position >= first, first, start)
        return start

    def relation(self, query_block, key_block):
        rows = self.half_rows
        low = self.doc_start(query_block * rows)
        high = self.doc_start(query_block * rows + rows - 1)
        visible = (key_block <= query_block) & (key_block * rows + rows - 1 >= low)
        whole = (key_block < query_block) & (key_block * rows >= high)
        return visible, whole

    def mask(self, query_block, key_block, query_dim):
        rows = self.half_rows
        query_pos = query_block * rows + lax.broadcasted_iota(jnp.int32, (rows, rows), query_dim)
        key_pos = key_block * rows + lax.broadcasted_iota(jnp.int32, (rows, rows), 1 - query_dim)
        return (key_pos <= query_pos) & (key_pos >= self.doc_start(query_pos))


def rope_rows(info, tables, half, head_dim):
    base_cos, base_sin, step_cos, step_sin = tables
    block = info.block(info.ctx, half)
    return block_tables(
        base_cos[pl.ds(block, 1), :],
        base_sin[pl.ds(block, 1), :],
        step_cos[...],
        step_sin[...],
        head_dim,
    )


def project_kernel(devices, head_dim, info_ref, x_ref, gain_ref, wq_ref, wk_ref, wv_ref, qg_ref,
                   kg_ref, bc_ref, bs_ref, sc_ref, ss_ref, kv_ref, q_ref, raw_ref, n1_ref, x_out):
    rows = x_ref.shape[0] // 2
    info = Info(info_ref, devices, rows)
    tables = (bc_ref, bs_ref, sc_ref, ss_ref)
    chunks = wq_ref.shape[1] // LANES
    for half in range(2):
        here = slice(half * rows, half * rows + rows)
        from_row = pl.multiple_of(jnp.bitwise_xor(half, info.core) * rows, rows)
        x_low = x_ref[pl.ds(from_row, rows), :]
        x_out[here, :] = x_low
        normed = rms_norm(x_low.astype(F32), gain_ref[...]).astype(BF16)
        n1_ref[here, :] = normed
        cos, sin = rope_rows(info, tables, half, head_dim)

        def turned(raw, gain):
            unit = raw * lax.rsqrt(head_mean(raw * raw, head_dim) + EPS) * gain
            return unit * cos + swap_halves(unit, head_dim) * sin

        key_raw = matmul(normed, wk_ref[...])
        kv_ref[here, 0:LANES] = turned(key_raw, kg_ref[...]).astype(BF16)
        kv_ref[here, LANES : 2 * LANES] = matmul(normed, wv_ref[...]).astype(BF16)
        raw_ref[here, chunks * LANES : (chunks + 1) * LANES] = key_raw
        query_raw = matmul(normed, wq_ref[...])
        raw_ref[here, 0 : chunks * LANES] = query_raw
        for chunk in range(chunks):
            cols = slice(chunk * LANES, (chunk + 1) * LANES)
            q_ref[here, cols] = (turned(query_raw[:, cols], qg_ref[...]) * SCALE).astype(BF16)


def spread_heads(low, rows, half, head_dim, out_ref):
    here = slice(half * rows, half * rows + rows)
    groups = mix_low(low[here, 0:LANES], low[here, LANES : 2 * LANES], head_dim)
    lane = lane_index((rows, LANES))
    for kv in range(2):
        for group in range(2):
            at = (2 * kv + group) * rows
            out_ref[half, at : at + rows, :] = jnp.where(
                lane // head_dim == kv, groups[group].astype(F32), 0.0
            ).astype(BF16)


def join_heads(stacked, rows, head_dim):
    lane = lane_index((rows, LANES))
    groups = [
        jnp.where(
            lane < head_dim,
            stacked[group * rows : (group + 1) * rows],
            stacked[(2 + group) * rows : (3 + group) * rows],
        )
        for group in range(2)
    ]
    return mix_heads(groups[0], groups[1], head_dim)


def fetch_slots(slot_refs, held, sems):
    copies = [
        pltpu.make_async_copy(ref, held.at[at], sems.at[at]) for at, ref in enumerate(slot_refs)
    ]
    for copy in copies:
        copy.start()
    return copies


def attend_kernel(devices, head_dim, info_ref, q_ref, *refs):
    slots = refs[:devices]
    o_ref, o32_ref, lse_ref, held, spread, total, sems = refs[devices:]
    rows = q_ref.shape[0] // 2
    info = Info(info_ref, devices, rows)
    copies = fetch_slots(slots, held, sems)
    q_low = q_ref[...]
    for half in range(2):
        spread_heads(q_low, rows, half, head_dim, spread)
    total[...] = jnp.zeros_like(total)
    for copy in copies:
        copy.wait()

    def one_key_block(step, carry):
        slot, key_half = step // 2, lax.rem(step, 2)
        key_block = info.block(info.slot_source(slot), key_half)
        key_rows = pl.ds(pl.multiple_of(key_half * rows, rows), rows)
        for half in range(2):
            query_block = info.block(info.ctx, half)
            visible, whole = info.relation(query_block, key_block)

            def take(masked, half=half, query_block=query_block):
                keys = held[slot, key_rows, 0:LANES]
                values = jnp.concatenate(
                    [held[slot, key_rows, LANES : 2 * LANES], jnp.ones((rows, LANES), BF16)], axis=1
                )
                if masked:
                    allowed = info.mask(query_block, key_block, 0)
                for part in range(4):
                    at = slice(part * rows, part * rows + rows)
                    scores = contract(spread[half, at, :], keys, 1, 1)
                    if masked:
                        scores = jnp.where(allowed, scores, NEG)
                    weights = jnp.exp(scores).astype(BF16)
                    total[half, at, :] += matmul(weights, values)

            pl.when(visible & whole)(functools.partial(take, False))
            pl.when(visible & jnp.logical_not(whole))(functools.partial(take, True))
        return carry

    lax.fori_loop(0, 2 * devices, one_key_block, 0)
    for half in range(2):
        here = slice(half * rows, half * rows + rows)
        sums = total[half, :, LANES : 2 * LANES]
        chunks = join_heads(total[half, :, 0:LANES] / sums, rows, head_dim)
        for chunk in range(2):
            cols = slice(chunk * LANES, (chunk + 1) * LANES)
            o32_ref[here, cols] = chunks[chunk]
            o_ref[here, cols] = chunks[chunk].astype(BF16)
        lse_ref[half] = jnp.transpose(jnp.log(sums))[0:8, :]


def attend_back_kernel(devices, head_dim, info_ref, q_ref, do_ref, o32_ref, lse_ref, raw_ref, qg_ref,
                       bc_ref, bs_ref, sc_ref, ss_ref, *refs):
    slots = refs[:devices]
    same_ref, other_ref, dq_ref, gain_ref, held, spread, spread_do, delta, dq_t, dkv, sems = refs[
        devices:
    ]
    rows = q_ref.shape[0] // 2
    pairs = devices // 2
    info = Info(info_ref, devices, rows)
    copies = fetch_slots(slots, held, sems)
    q_low, do_low = q_ref[...], do_ref[...]
    for half in range(2):
        here = slice(half * rows, half * rows + rows)
        spread_heads(q_low, rows, half, head_dim, spread)
        spread_heads(do_low, rows, half, head_dim, spread_do)
        product = do_low[here, :].astype(F32) * o32_ref[here, :]
        for chunk in range(2):
            turned = jnp.transpose(product[:, chunk * LANES : (chunk + 1) * LANES])
            for group in range(2):
                at = (2 * chunk + group) * rows
                delta[half, :, at : at + rows] = jnp.broadcast_to(
                    jnp.sum(
                        turned[group * head_dim : (group + 1) * head_dim], axis=0, keepdims=True
                    ),
                    (8, rows),
                )
    dq_t[...] = jnp.zeros_like(dq_t)
    for copy in copies:
        copy.wait()

    def one_key_block(step, carry):
        slot, key_half = step // 2, lax.rem(step, 2)
        key_block = info.block(info.slot_source(slot), key_half)
        key_rows = pl.ds(pl.multiple_of(key_half * rows, rows), rows)
        dkv[...] = jnp.zeros_like(dkv)
        for half in range(2):
            query_block = info.block(info.ctx, half)
            visible, whole = info.relation(query_block, key_block)

            def take(masked, half=half, query_block=query_block):
                keys = held[slot, key_rows, 0:LANES]
                values = held[slot, key_rows, LANES : 2 * LANES]
                if masked:
                    allowed = info.mask(query_block, key_block, 1)
                for part in range(4):
                    at = slice(part * rows, part * rows + rows)
                    queries, grads = spread[half, at, :], spread_do[half, at, :]
                    scores = contract(keys, queries, 1, 1) - lse_ref[half, 0:1, at]
                    if masked:
                        scores = jnp.where(allowed, scores, NEG)
                    probs = jnp.exp(scores)
                    grad_probs = contract(values, grads, 1, 1)
                    grad_scores = (probs * (grad_probs - delta[half, 0:1, at])).astype(BF16)
                    dkv[:, LANES : 2 * LANES] += matmul(probs.astype(BF16), grads)
                    dkv[:, 0:LANES] += matmul(grad_scores, queries)
                    dq_t[half, :, at] += contract(keys, grad_scores, 0, 0)

            pl.when(visible & whole)(functools.partial(take, False))
            pl.when(visible & jnp.logical_not(whole))(functools.partial(take, True))
        result = dkv[...].astype(BF16)

        @pl.when(slot < pairs)
        def _():
            same_ref[slot, key_rows, :] = result

        @pl.when(slot >= pairs)
        def _():
            other_ref[slot - pairs, key_rows, :] = result

        return carry

    lax.fori_loop(0, 2 * devices, one_key_block, 0)
    gain_sum = jnp.zeros((1, LANES), F32)
    for half in range(2):
        here = slice(half * rows, half * rows + rows)
        cos, sin = rope_rows(info, (bc_ref, bs_ref, sc_ref, ss_ref), half, head_dim)
        chunks = join_heads(jnp.transpose(dq_t[half]), rows, head_dim)
        for chunk in range(2):
            cols = slice(chunk * LANES, (chunk + 1) * LANES)
            grad = chunks[chunk] * SCALE
            grad = grad * cos - swap_halves(grad, head_dim) * sin
            back, term = head_norm_back(raw_ref[here, cols], qg_ref[...], grad, head_dim)
            dq_ref[here, cols] = back.astype(BF16)
            gain_sum += term
    gain_ref[...] = gain_sum


def key_back_kernel(devices, head_dim, count, info_ref, raw_ref, kg_ref, bc_ref, bs_ref, sc_ref,
                    ss_ref, *refs):
    parts = refs[:count]
    dk_ref, dv_ref, gain_ref = refs[count:]
    rows = raw_ref.shape[0] // 2
    info = Info(info_ref, devices, rows)
    gain_sum = jnp.zeros((1, LANES), F32)
    for half in range(2):
        here = slice(half * rows, half * rows + rows)
        grad = sum(part[here, :].astype(F32) for part in parts)
        dv_ref[here, :] = grad[:, LANES : 2 * LANES].astype(BF16)
        cos, sin = rope_rows(info, (bc_ref, bs_ref, sc_ref, ss_ref), half, head_dim)
        grad_k = grad[:, 0:LANES]
        grad_k = grad_k * cos - swap_halves(grad_k, head_dim) * sin
        back, term = head_norm_back(
            raw_ref[here, 2 * LANES : 3 * LANES], kg_ref[...], grad_k, head_dim
        )
        dk_ref[here, :] = back.astype(BF16)
        gain_sum += term
    gain_ref[...] = gain_sum


def call_kernel(body, outs, operands, memory, scratch=(), flops=10**9):
    kinds = {
        "s": pl.BlockSpec(memory_space=pltpu.SMEM),
        "v": pl.BlockSpec(memory_space=pltpu.VMEM),
        "a": pl.BlockSpec(memory_space=pl.ANY),
    }
    return pl.pallas_call(
        body,
        out_shape=[jax.ShapeDtypeStruct(shape, kind) for shape, kind in outs],
        in_specs=[kinds[m] for m in memory],
        out_specs=[kinds["v"]] * len(outs),
        scratch_shapes=list(scratch),
        compiler_params=pltpu.CompilerParams(vmem_limit_bytes=VMEM_LIMIT),
        cost_estimate=pl.CostEstimate(flops=flops, bytes_accessed=4 * 10**6, transcendentals=0),
    )(*operands)


def flip(values, axis, bit):
    size = lax.axis_size(axis)
    return lax.ppermute(values, axis, [(i, i ^ bit) for i in range(size)])


def shift(values, step):
    size = lax.axis_size("ctx")
    return lax.ppermute(values, "ctx", [(i, (i + step) % size) for i in range(size)])


def gather_slots(values):
    pairs = lax.axis_size("ctx") // 2
    same = [values] + [shift(values, 2 * k) for k in range(1, pairs)]
    return same + [flip(part, "ctx", 1) for part in same]


def wt_sum(mine, other):
    chip = (mine.astype(F32) + flip(other, "wt", 1).astype(F32)).astype(BF16)
    whole = (chip.astype(F32) + flip(chip, "wt", 2).astype(F32)).astype(BF16)
    return whole, flip(whole, "wt", 1)


def ctx_scatter(values):
    devices = lax.axis_size("ctx")
    pairs = devices // 2
    index = lax.axis_index("ctx")
    column, row = index % 2, index // 2
    split = values.reshape((pairs, 2) + values.shape[1:])
    sent = lax.dynamic_index_in_dim(split, 1 - column, 1, keepdims=False)
    kept = lax.dynamic_index_in_dim(split, column, 1, keepdims=False)
    both = (kept.astype(F32) + flip(sent, "ctx", 1).astype(F32)).astype(values.dtype)
    total = lax.dynamic_index_in_dim(both, row, 0, keepdims=False).astype(F32)
    for k in range(1, pairs):
        piece = lax.dynamic_index_in_dim(both, (row - k + pairs) % pairs, 0, keepdims=False)
        total = total + shift(piece, -2 * k).astype(F32)
    return total


def on_device(
    block_in,
    doc_ids,
    block_of,
    w_query,
    w_key,
    w_value,
    w_out,
    w_gate,
    w_up,
    w_down,
    attn_gain,
    ffn_gain,
    query_gain,
    key_gain,
    cotangent,
):
    tok_rows, width = block_in.shape
    half_rows = tok_rows // 2
    head_dim = query_gain.shape[0]
    q_width, kv_width = w_query.shape[1], w_key.shape[1]
    devices = lax.axis_size("ctx")
    pairs = devices // 2
    blocks = block_of.shape[0]
    wt_count = lax.axis_size("wt")
    core = lax.axis_index("wt") % 2

    starts = [jnp.sum((doc_ids < doc).astype(jnp.int32)) for doc in range(1, DOCS)]
    info = jnp.concatenate(
        [jnp.stack([lax.axis_index("ctx"), core] + starts).astype(jnp.int32), block_of]
    )
    half_dim = head_dim // 2
    freqs = THETA ** (-2.0 * (np.arange(LANES) % half_dim).astype(np.float64) / head_dim)
    base_angle = (np.arange(blocks) * half_rows)[:, None] * freqs[None, :]
    step_angle = np.arange(half_rows)[:, None] * freqs[None, :]
    tables = [
        jnp.asarray(table.astype(np.float32))
        for table in (np.cos(base_angle), np.sin(base_angle), np.cos(step_angle), np.sin(step_angle))
    ]
    query_gain_row = jnp.tile(query_gain, LANES // head_dim)[None, :]
    key_gain_row = jnp.tile(key_gain, LANES // head_dim)[None, :]

    def to_local(values):
        return jnp.where(core == 0, values, jnp.roll(values, half_rows, 0))

    def from_local(mine, other):
        return jnp.concatenate(
            [jnp.where(core == 0, mine, other), jnp.where(core == 0, other, mine)], axis=0
        )

    key_value, query, raw, normed_one, x_local = call_kernel(
        functools.partial(project_kernel, devices, head_dim),
        [
            ((tok_rows, 2 * kv_width), BF16),
            ((tok_rows, q_width), BF16),
            ((tok_rows, q_width + kv_width), F32),
            ((tok_rows, width), BF16),
            ((tok_rows, width), BF16),
        ],
        [info, block_in, attn_gain[None, :], w_query, w_key, w_value, query_gain_row, key_gain_row]
        + tables,
        "s" + "v" * 11,
    )
    slots = gather_slots(key_value)
    out_grad = to_local(cotangent)
    grad_hidden = contract(out_grad, w_down, 1, 1)
    scratch_kv = pltpu.VMEM((devices, tok_rows, 2 * kv_width), BF16)
    stacked = 4 * half_rows
    out_low, out_wide, log_total = call_kernel(
        functools.partial(attend_kernel, devices, head_dim),
        [
            ((tok_rows, q_width), BF16),
            ((tok_rows, q_width), F32),
            ((2, 8, stacked), F32),
        ],
        [info, query] + slots,
        "sv" + "a" * devices,
        [
            scratch_kv,
            pltpu.VMEM((2, stacked, LANES), BF16),
            pltpu.VMEM((2, stacked, 2 * LANES), F32),
            pltpu.SemaphoreType.DMA((devices,)),
        ],
        flops=8 * 10**9,
    )
    attn_other = matmul(out_low[half_rows:], w_out).astype(BF16)
    attn_mine = matmul(out_low[:half_rows], w_out).astype(BF16)
    attn_sum = jnp.concatenate(wt_sum(attn_mine, attn_other), axis=0)
    inputs = x_local.astype(F32)
    middle = inputs + attn_sum.astype(F32)
    normed_two = rms_norm(middle, ffn_gain).astype(BF16)
    gate_proj = matmul(normed_two, w_gate)
    up_proj = matmul(normed_two, w_up)
    sigmoid_gate = jax.nn.sigmoid(gate_proj)
    silu_gate = gate_proj * sigmoid_gate
    hidden = (silu_gate * up_proj).astype(BF16)
    grad_gate = (
        grad_hidden * up_proj * sigmoid_gate * (1.0 + gate_proj * (1.0 - sigmoid_gate))
    ).astype(BF16)
    grad_upper = (grad_hidden * silu_gate).astype(BF16)

    def normed_two_part(here):
        return (
            contract(grad_gate[here], w_gate, 1, 1) + contract(grad_upper[here], w_up, 1, 1)
        ).astype(BF16)

    mine, other = slice(0, half_rows), slice(half_rows, tok_rows)
    n2_other = normed_two_part(other)
    n2_mine = normed_two_part(mine)
    normed_two_grad = jnp.concatenate(wt_sum(n2_mine, n2_other), axis=0).astype(F32)

    def by_device(grad):
        return grad.astype(BF16).reshape((devices, grad.shape[0] // devices) + grad.shape[1:])

    grad_w_down = ctx_scatter(by_device(contract(out_grad, hidden, 0, 0)))
    grad_w_gate = ctx_scatter(by_device(contract(normed_two, grad_gate, 0, 0)))
    grad_w_up = ctx_scatter(by_device(contract(normed_two, grad_upper, 0, 0)))

    middle_back, ffn_gain_terms = norm_back(middle, ffn_gain, normed_two_grad)
    grad_middle = out_grad.astype(F32) + middle_back
    grad_middle_low = grad_middle.astype(BF16)
    grad_attended = contract(grad_middle_low, w_out, 1, 1).astype(BF16)
    grad_same, grad_other, query_raw_low, query_gain_sum = call_kernel(
        functools.partial(attend_back_kernel, devices, head_dim),
        [
            ((pairs, tok_rows, 2 * kv_width), BF16),
            ((pairs, tok_rows, 2 * kv_width), BF16),
            ((tok_rows, q_width), BF16),
            ((1, LANES), F32),
        ],
        [info, query, grad_attended, out_wide, log_total, raw, query_gain_row] + tables + slots,
        "s" + "v" * 10 + "a" * devices,
        [
            scratch_kv,
            pltpu.VMEM((2, stacked, LANES), BF16),
            pltpu.VMEM((2, stacked, LANES), BF16),
            pltpu.VMEM((2, 8, stacked), F32),
            pltpu.VMEM((2, LANES, stacked), F32),
            pltpu.VMEM((half_rows, 2 * LANES), F32),
            pltpu.SemaphoreType.DMA((devices,)),
        ],
        flops=16 * 10**9,
    )
    hidden_late, normed_two_late = lax.optimization_barrier((hidden, normed_two_grad))
    ffn_other = matmul(hidden_late[other], w_down).astype(BF16)
    ffn_mine = matmul(hidden_late[mine], w_down).astype(BF16)
    ffn_mine, ffn_other = wt_sum(ffn_mine, ffn_other)
    block_out = from_local(
        (middle[mine] + ffn_mine.astype(F32)).astype(BF16),
        (middle[other] + ffn_other.astype(F32)).astype(BF16),
    )

    both = (grad_same.astype(F32) + flip(grad_other, "ctx", 1).astype(F32)).astype(BF16)
    key_value_parts = [both[0]] + [shift(both[k], -2 * k) for k in range(1, pairs)]
    key_raw_low, value_raw_low, key_gain_sum = call_kernel(
        functools.partial(key_back_kernel, devices, head_dim, pairs),
        [
            ((tok_rows, kv_width), BF16),
            ((tok_rows, kv_width), BF16),
            ((1, LANES), F32),
        ],
        [info, raw, key_gain_row] + tables + key_value_parts,
        "s" + "v" * (6 + pairs),
    )
    normed_one_part = (
        contract(query_raw_low, w_query, 1, 1)
        + contract(key_raw_low, w_key, 1, 1)
        + contract(value_raw_low, w_value, 1, 1)
    )
    part_low = normed_one_part.astype(BF16)
    n1_mine, n1_other = wt_sum(part_low[mine], part_low[other])
    normed_one_grad = jnp.concatenate([n1_mine, n1_other], axis=0).astype(F32)

    inverse_one = lax.rsqrt(jnp.mean(inputs * inputs, axis=-1, keepdims=True) + EPS)
    attn_gain_part = jnp.sum(normed_one_part * inputs * inverse_one, axis=0)
    ffn_gain_part = jnp.sum(ffn_gain_terms, axis=0) * (1.0 / wt_count)

    def fold(row):
        return jnp.sum(row.reshape(LANES // head_dim, head_dim), axis=0)

    gains = jnp.concatenate(
        [
            part.reshape(devices, part.shape[0] // devices)
            for part in (attn_gain_part, ffn_gain_part, fold(query_gain_sum), fold(key_gain_sum))
        ],
        axis=1,
    )
    gains = gains + flip(gains, "wt", 1)
    gains = gains + flip(gains, "wt", 2)
    gains = ctx_scatter(gains)
    gain_width, head_width = width // devices, head_dim // devices

    grad_w_out = ctx_scatter(by_device(contract(grad_middle_low, out_low, 0, 0)))
    grad_w_qkv = ctx_scatter(
        by_device(
            contract(
                normed_one,
                jnp.concatenate([query_raw_low, key_raw_low, value_raw_low], axis=1),
                0,
                0,
            )
        )
    )
    input_back, _ = norm_back(inputs, attn_gain, normed_one_grad)
    grad_input = grad_middle + input_back
    return (
        block_out,
        from_local(grad_input[mine], grad_input[other]),
        grad_w_qkv[:, :q_width],
        grad_w_qkv[:, q_width : q_width + kv_width],
        grad_w_qkv[:, q_width + kv_width :],
        grad_w_out.T,
        grad_w_gate,
        grad_w_up,
        grad_w_down.T,
        gains[:gain_width],
        gains[gain_width : 2 * gain_width],
        gains[2 * gain_width : 2 * gain_width + head_width],
        gains[2 * gain_width + head_width :],
    )


def solution(mesh):
    in_specs = (
        P("ctx", None),
        P(),
        P(),
        P(None, "wt"),
        P(None, "wt"),
        P(None, "wt"),
        P("wt", None),
        P(None, "wt"),
        P(None, "wt"),
        P("wt", None),
        P(),
        P(),
        P(),
        P(),
        P("ctx", None),
    )
    out_specs = (
        P("ctx", None),
        P("ctx", None),
        P("ctx", "wt"),
        P("ctx", "wt"),
        P("ctx", "wt"),
        P("wt", "ctx"),
        P("ctx", "wt"),
        P("ctx", "wt"),
        P("wt", "ctx"),
        P("ctx"),
        P("ctx"),
        P("ctx"),
        P("ctx"),
    )
    return jax.shard_map(
        on_device, mesh=mesh, in_specs=in_specs, out_specs=out_specs, check_vma=False
    )
```

time: 1290 us -> 383 us (0.30)
  waiting for transfers between devices: 713 us -> 162 us
  other arithmetic: 203 us -> 41 us
  local copies, waits for them, and re-layouts: 176 us -> 27.5 us
  starting transfers between devices: 0.98 us -> 84.8 us
  matrix products: 95.7 us -> 31.4 us
  loops' own time: 42.7 us -> 0 us
  Pallas kernels: 0 us -> 28.9 us
  blocking collectives: 27.3 us -> 0 us
  between operations: 15.8 us -> 1.71 us
    reduce_scatter x7 -> x0, waiting for transfers between devices: 431 us -> none  [the longest x1 69.8 us: on_device(): lax.psum_scatter(grad_w_up.astype(jnp.bfloat16), 'ctx', scatter_dimension...]
    ppermute x0 -> x49, waiting for transfers between devices: none -> 162 us  [the longest x25 106 us: flip(): return lax.ppermute(values, axis, [(i, i ^ bit) for i in range(size)])]
    psum x3 -> x0, waiting for transfers between devices: 140 us -> none  [the longest x1 52.1 us: on_device(): lax.psum(matmul(hidden, w_down).astype(jnp.bfloat16), 'wt')]
    unnamed x16 -> x0, waiting for transfers between devices: 95.5 us -> none
    ppermute x0 -> x49, starting transfers between devices: none -> 84.8 us  [the longest x24 43.9 us: shift(): lax.ppermute(values, 'ctx', [(i, (i + step) % size) for i in range(size)])]
    reduce_or x32 -> x0, other arithmetic: 82.3 us -> none  [tile_visible(): jnp.any((query_pos >= first_pos) & (query_doc >= doc_low) & (query_doc <=...]
    dynamic_slice x87 -> x6, local copies, waits for them, and re-layouts: 76.5 us -> 5.6 us  [the longest x2 3.21 us: ctx_scatter(): sent = lax.dynamic_index_in_dim(split, 1 - column, 1, keepdims=False)]
    dot_general x84 -> x20, matrix products: 95.7 us -> 31.4 us  [the longest x14 21.2 us: contract(): lax.dot_general(left, right, (((left_dim,), (right_dim,)), ((), ())), pre...]
  transfers between devices with their start and end apart: 14 -> 49, of which waited for: 14 -> 22; matrix products, arithmetic and copies ran while one was open for 8% -> 17% of each run, Pallas kernels for 0% -> 4%
where the time goes in v1:
time: 383 us; the launch traced here: 377 us
  waiting for transfers between devices  162 us (42%)
  starting transfers between devices  84.8 us (22%)
  other arithmetic  41 us (11%)
  matrix products  31.4 us (8%)
  Pallas kernels  28.9 us (8%)
  local copies, waits for them, and re-layouts  27.5 us (7%)
    ppermute x25, waiting for transfers between devices, flip(): return lax.ppermute(values, axis, [(i, i ^ bit) for i in range(size)])  106 us
    ppermute x24, waiting for transfers between devices, shift(): lax.ppermute(values, 'ctx', [(i, (i + step) % size) for i in range(size)])  55.9 us
    ppermute x24, starting transfers between devices, shift(): lax.ppermute(values, 'ctx', [(i, (i + step) % size) for i in range(size)])  43.9 us
    ppermute x25, starting transfers between devices, flip(): return lax.ppermute(values, axis, [(i, i ^ bit) for i in range(size)])  40.9 us
    pallas_call x4, Pallas kernels, call_kernel(): pl.pallas_call(body, out_shape=[jax.ShapeDtypeStruct(shape, kind) for sha...  28.9 us
    dot_general x14, matrix products, contract(): lax.dot_general(left, right, (((left_dim,), (right_dim,)), ((), ())), pre...  21.2 us
    dot_general x6, matrix products, matmul(): return jnp.dot(left, right, preferred_element_type=F32)  10.2 us
  transfers between devices with their start and end apart: 49, of which 22 were waited for; matrix products, arithmetic and copies ran while one was open for 17% of the time, Pallas kernels for 4%

profile of v1, /device:TPU:0, one launch (start us, length us, event | category | flops | bytes accessed | tf_op | source)
XLA Modules:
  0.0 377.4 jit_solution(4663587713621100732)
XLA Ops:
  7.9 4.8 %shard_map.282 = (bf16[512,256]{1,0:T(8,128)(2,1)}, bf16[512,256]{1,0:T(8,128)(2,1)}, f32[512,384]{1,0:T(8,128)}, bf16[512,1024]{1,0:T(8,128)(2,1)}, bf16[512,1024]{1,0:T(8,128)(2,1)}) custom-call(s32[21]{0:T(128)} %concatenate.28.info_ref, bf16[512,1024]{1,0:T(8,128)(2,1)} %x_ref.1, f32[1,1024]{1,0:T(1,128)} %bitcast.146, bf16[1024,256]{1,0:T(8,128)(2,1)} %wq_ref.1, ...), custom_call_target="tpu_custom_call" | custom-call | flops 1000000000 | bytes 4000000 | tf_op jit(solution)/shard_map/pallas_call | solution.py:375
  21.2 4.1 %collective-permute-done.refs_1_ = bf16[512,256]{1,0:T(8,128)(2,1)S(1)} collective-permute-done((bf16[512,256]{1,0:T(8,128)(2,1)}, bf16[512,256]{1,0:T(8,128)(2,1)S(1)}, u32[]{:S(2)}, u32[]{:S(2)}) %collective-permute-start) | collective-permute-done | bytes 262176 | tf_op jit(solution)/shard_map/ppermute | solution.py:393
  27.1 8.6 %collective-permute-done.1.refs_2_ = bf16[512,256]{1,0:T(8,128)(2,1)S(1)} collective-permute-done((bf16[512,256]{1,0:T(8,128)(2,1)}, bf16[512,256]{1,0:T(8,128)(2,1)S(1)}, u32[]{:S(2)}, u32[]{:S(2)}) %collective-permute-start.1) | collective-permute-done | bytes 262176 | tf_op jit(solution)/shard_map/ppermute | solution.py:393
  37.7 7.1 %collective-permute-done.5.refs_6_ = bf16[512,256]{1,0:T(8,128)(2,1)S(1)} collective-permute-done((bf16[512,256]{1,0:T(8,128)(2,1)S(1)}, bf16[512,256]{1,0:T(8,128)(2,1)S(1)}, u32[]{:S(2)}, u32[]{:S(2)}) %collective-permute-start.5) | collective-permute-done | bytes 262176 | tf_op jit(solution)/shard_map/ppermute | solution.py:388
  44.9 4.6 %collective-permute-done.6.refs_7_ = bf16[512,256]{1,0:T(8,128)(2,1)S(1)} collective-permute-done((bf16[512,256]{1,0:T(8,128)(2,1)S(1)}, bf16[512,256]{1,0:T(8,128)(2,1)S(1)}, u32[]{:S(2)}, u32[]{:S(2)}) %collective-permute-start.6) | collective-permute-done | bytes 262176 | tf_op jit(solution)/shard_map/ppermute | solution.py:388
  50.2 8.1 %shard_map.283 = (bf16[512,256]{1,0:T(8,128)(2,1)}, f32[512,256]{1,0:T(8,128)}, f32[2,8,1024]{2,1,0:T(8,128)}) custom-call(s32[21]{0:T(128)} %concatenate.28.info_ref, bf16[512,256]{1,0:T(8,128)(2,1)} %get-tuple-element.30.q_ref, bf16[512,256]{1,0:T(8,128)(2,1)} %get-tuple-element.31.refs_0_, bf16[512,256]{1,0:T(8,128)(2,1)} %copy-done.35, ...), custom_call_target="tpu_custom_call" | custom-call | flops 8000000000 | bytes 4000000 | tf_op jit(solution)/shard_map/pallas_call | solution.py:375
  65.1 12.7 %collective-permute-done.8 = bf16[256,1024]{1,0:T(8,128)(2,1)} collective-permute-done((bf16[256,1024]{1,0:T(8,128)(2,1)}, bf16[256,1024]{1,0:T(8,128)(2,1)}, u32[]{:S(2)}, u32[]{:S(2)}) %collective-permute-start.8) | collective-permute-done | bytes 524320 | tf_op jit(solution)/shard_map/ppermute | solution.py:388
  104.3 7.6 %collective-permute-start.39 = (bf16[4,128,1152]{1,2,0:T(8,128)(2,1)}, bf16[4,128,1152]{1,2,0:T(8,128)(2,1)}, u32[]{:S(2)}, u32[]{:S(2)}) collective-permute-start(bf16[4,128,1152]{1,2,0:T(8,128)(2,1)} %bitcast.140), channel_id=1, source_target_pairs={{0,4},{4,0},{8,12},{12,8},{16,20},{20,16},{24,28},{28,24},{1,5},{5... | collective-permute-start | bytes 3538952 | tf_op jit(solution)/shard_map/ppermute | solution.py:388
  128.9 10.1 %collective-permute-done.11 = bf16[256,1024]{1,0:T(8,128)(2,1)S(1)} collective-permute-done((bf16[256,1024]{1,0:T(8,128)(2,1)S(1)}, bf16[256,1024]{1,0:T(8,128)(2,1)S(1)}, u32[]{:S(2)}, u32[]{:S(2)}) %collective-permute-start.11) | collective-permute-done | bytes 524320 | tf_op jit(solution)/shard_map/ppermute | solution.py:388
  139.3 10.6 %collective-permute-done.14 = bf16[256,1024]{1,0:T(8,128)(2,1)S(1)} collective-permute-done((bf16[256,1024]{1,0:T(8,128)(2,1)S(1)}, bf16[256,1024]{1,0:T(8,128)(2,1)S(1)}, u32[]{:S(2)}, u32[]{:S(2)}) %collective-permute-start.14) | collective-permute-done | bytes 524320 | tf_op jit(solution)/shard_map/ppermute | solution.py:388
  153.1 11.0 %collective-permute-done.35 = bf16[4,128,1152]{2,1,0:T(8,128)(2,1)S(1)} collective-permute-done((bf16[4,128,1152]{2,1,0:T(8,128)(2,1)S(1)}, bf16[4,128,1152]{2,1,0:T(8,128)(2,1)S(1)}, u32[]{:S(2)}, u32[]{:S(2)}) %collective-permute-start.35) | collective-permute-done | bytes 1179680 | tf_op jit(solution)/shard_map/ppermute | solution.py:388
  164.4 24.3 %collective-permute-done.31 = bf16[4,128,1152]{2,1,0:T(8,128)(2,1)S(1)} collective-permute-done((bf16[4,128,1152]{2,1,0:T(8,128)(2,1)S(1)}, bf16[4,128,1152]{2,1,0:T(8,128)(2,1)S(1)}, u32[]{:S(2)}, u32[]{:S(2)}) %collective-permute-start.31) | collective-permute-done | bytes 1179680 | tf_op jit(solution)/shard_map/ppermute | solution.py:388
  188.7 3.6 collective-permute-start.42
  195.4 5.1 %collective-permute-done.42 = bf16[128,1152]{0,1:T(8,128)(2,1)S(1)} collective-permute-done((bf16[128,1152]{0,1:T(8,128)(2,1)S(1)}, bf16[128,1152]{0,1:T(8,128)(2,1)S(1)}, u32[]{:S(2)}, u32[]{:S(2)}) %collective-permute-start.42) | collective-permute-done | bytes 294944 | tf_op jit(solution)/shard_map/ppermute | solution.py:393
  206.2 4.3 %collective-permute-start.32 = (bf16[128,1152]{1,0:T(8,128)(2,1)}, bf16[128,1152]{1,0:T(8,128)(2,1)}, u32[]{:S(2)}, u32[]{:S(2)}) collective-permute-start(bf16[128,1152]{1,0:T(8,128)(2,1)} %get-tuple-element.74), channel_id=1, source_target_pairs={{0,24},{4,28},{8,0},{12,4},{16,8},{20,12},{24,16},{28,20},{1,25},{... | collective-permute-start | bytes 884744 | tf_op jit(solution)/shard_map/ppermute | solution.py:393
  210.5 15.4 %collective-permute-done.37 = bf16[128,1152]{1,0:T(8,128)(2,1)S(1)} collective-permute-done((bf16[128,1152]{1,0:T(8,128)(2,1)S(1)}, bf16[128,1152]{1,0:T(8,128)(2,1)S(1)}, u32[]{:S(2)}, u32[]{:S(2)}) %collective-permute-start.37) | collective-permute-done | bytes 294944 | tf_op jit(solution)/shard_map/ppermute | solution.py:393
  225.9 11.8 %collective-permute-start.34 = (bf16[128,1152]{1,0:T(8,128)(2,1)}, bf16[128,1152]{1,0:T(8,128)(2,1)}, u32[]{:S(2)}, u32[]{:S(2)}) collective-permute-start(bf16[128,1152]{1,0:T(8,128)(2,1)} %get-tuple-element.75), channel_id=1, source_target_pairs={{0,8},{4,12},{8,16},{12,20},{16,24},{20,28},{24,0},{28,4},{1,9},{5... | collective-permute-start | bytes 884744 | tf_op jit(solution)/shard_map/ppermute | solution.py:393
  245.6 13.3 %shard_map.284 = (bf16[4,512,256]{2,1,0:T(8,128)(2,1)}, bf16[4,512,256]{2,1,0:T(8,128)(2,1)}, bf16[512,256]{1,0:T(8,128)(2,1)}, f32[1,128]{1,0:T(1,128)}) custom-call(s32[21]{0:T(128)} %concatenate.28.info_ref, bf16[512,256]{1,0:T(8,128)(2,1)} %get-tuple-element.30.q_ref, bf16[512,256]{1,0:T(8,128)(2,1)} %convolution_convert_fusion.9.do_ref, ...), custom_call_target="tpu_custom_call" | custom-call | flops 16000000000 | bytes 4000000 | tf_op jit(solution)/shard_map/pallas_call | solution.py:375
  258.9 14.1 %collective-permute-start.16 = (bf16[4,512,256]{2,1,0:T(8,128)(2,1)}, bf16[4,512,256]{2,1,0:T(8,128)(2,1)S(1)}, u32[]{:S(2)}, u32[]{:S(2)}) collective-permute-start(bf16[4,512,256]{2,1,0:T(8,128)(2,1)} %get-tuple-element.39), channel_id=1, source_target_pairs={{0,4},{4,0},{8,12},{12,8},{16,20},{20,16},{24,28},{28,24},{1,5},{5... | collective-permute-start | bytes 3145736 | tf_op jit(solution)/shard_map/ppermute | solution.py:388
  278.9 14.1 %collective-permute-done.16 = bf16[4,512,256]{2,1,0:T(8,128)(2,1)S(1)} collective-permute-done((bf16[4,512,256]{2,1,0:T(8,128)(2,1)}, bf16[4,512,256]{2,1,0:T(8,128)(2,1)S(1)}, u32[]{:S(2)}, u32[]{:S(2)}) %collective-permute-start.16) | collective-permute-done | bytes 1048608 | tf_op jit(solution)/shard_map/ppermute | solution.py:388
  294.3 3.9 %collective-permute-start.18 = (bf16[512,256]{1,0:T(8,128)(2,1)}, bf16[512,256]{1,0:T(8,128)(2,1)}, u32[]{:S(2)}, u32[]{:S(2)}) collective-permute-start(bf16[512,256]{1,0:T(8,128)(2,1)} %get-tuple-element.78), channel_id=1, source_target_pairs={{0,16},{4,20},{8,24},{12,28},{16,0},{20,4},{24,8},{28,12},{1,17},{... | collective-permute-start | bytes 786440 | tf_op jit(solution)/shard_map/ppermute | solution.py:393
  304.2 13.3 %collective-permute-done.18.refs_2_ = bf16[512,256]{1,0:T(8,128)(2,1)} collective-permute-done((bf16[512,256]{1,0:T(8,128)(2,1)}, bf16[512,256]{1,0:T(8,128)(2,1)}, u32[]{:S(2)}, u32[]{:S(2)}) %collective-permute-start.18) | collective-permute-done | bytes 262176 | tf_op jit(solution)/shard_map/ppermute | solution.py:393
  333.0 7.4 %collective-permute-done.23 = bf16[4,128,512]{2,1,0:T(8,128)(2,1)S(1)} collective-permute-done((bf16[4,128,512]{2,1,0:T(8,128)(2,1)S(1)}, bf16[4,128,512]{2,1,0:T(8,128)(2,1)S(1)}, u32[]{:S(2)}, u32[]{:S(2)}) %collective-permute-start.23) | collective-permute-done | bytes 524320 | tf_op jit(solution)/shard_map/ppermute | solution.py:388
  348.5 4.3 %collective-permute-done.25 = bf16[128,512]{1,0:T(8,128)(2,1)} collective-permute-done((bf16[128,512]{1,0:T(8,128)(2,1)S(1)}, bf16[128,512]{1,0:T(8,128)(2,1)}, u32[]{:S(2)}, u32[]{:S(2)}) %collective-permute-start.25) | collective-permute-done | bytes 131104 | tf_op jit(solution)/shard_map/ppermute | solution.py:393
  (269 shorter events, 151.3 us)
Async XLA Ops:
  15.8 19.9 %collective-permute-start.1 = (bf16[512,256]{1,0:T(8,128)(2,1)}, bf16[512,256]{1,0:T(8,128)(2,1)S(1)}, u32[]{:S(2)}, u32[]{:S(2)}) collective-permute-start(bf16[512,256]{1,0:T(8,128)(2,1)} %get-tuple-element.31.refs_0_), channel_id=1, source_target_pairs={{0,16},{4,20},{8,24},{12,28},{16,0},{20,4},{24,8},{28,12},{1,17},{... | collective-permute-start | bytes 786440 | tf_op jit(solution)/shard_map/ppermute | solution.py:393
  18.4 18.8 %collective-permute-start.2 = (bf16[512,256]{1,0:T(8,128)(2,1)}, bf16[512,256]{1,0:T(8,128)(2,1)S(1)}, u32[]{:S(2)}, u32[]{:S(2)}) collective-permute-start(bf16[512,256]{1,0:T(8,128)(2,1)} %get-tuple-element.31.refs_0_), channel_id=1, source_target_pairs={{0,24},{4,28},{8,0},{12,4},{16,8},{20,12},{24,16},{28,20},{1,25},{... | collective-permute-start | bytes 786440 | tf_op jit(solution)/shard_map/ppermute | solution.py:393
  19.7 18.0 %collective-permute-start.3 = (bf16[512,256]{1,0:T(8,128)(2,1)}, bf16[512,256]{1,0:T(8,128)(2,1)S(1)}, u32[]{:S(2)}, u32[]{:S(2)}) collective-permute-start(bf16[512,256]{1,0:T(8,128)(2,1)} %get-tuple-element.31.refs_0_), channel_id=1, source_target_pairs={{0,4},{4,0},{8,12},{12,8},{16,20},{20,16},{24,28},{28,24},{1,5},{5... | collective-permute-start | bytes 786440 | tf_op jit(solution)/shard_map/ppermute | solution.py:388
  63.5 14.3 %collective-permute-start.8 = (bf16[256,1024]{1,0:T(8,128)(2,1)}, bf16[256,1024]{1,0:T(8,128)(2,1)}, u32[]{:S(2)}, u32[]{:S(2)}) collective-permute-start(bf16[256,1024]{1,0:T(8,128)(2,1)} %fusion.14), channel_id=1, source_target_pairs={{0,2},{1,3},{2,0},{3,1},{4,6},{5,7},{6,4},{7,5},{8,10},{9,11},{10,... | collective-permute-start | bytes 1572872 | tf_op jit(solution)/shard_map/ppermute | solution.py:388
  99.8 21.4 %collective-permute-start.10 = (bf16[256,1024]{1,0:T(8,128)(2,1)}, bf16[256,1024]{1,0:T(8,128)(2,1)}, u32[]{:S(2)}, u32[]{:S(2)}) collective-permute-start(bf16[256,1024]{1,0:T(8,128)(2,1)} %fusion.17), channel_id=1, source_target_pairs={{0,1},{1,0},{2,3},{3,2},{4,5},{5,4},{6,7},{7,6},{8,9},{9,8},{10,11... | collective-permute-start | bytes 1572872 | tf_op jit(solution)/shard_map/ppermute | solution.py:388
  104.3 45.9 %collective-permute-start.39 = (bf16[4,128,1152]{1,2,0:T(8,128)(2,1)}, bf16[4,128,1152]{1,2,0:T(8,128)(2,1)}, u32[]{:S(2)}, u32[]{:S(2)}) collective-permute-start(bf16[4,128,1152]{1,2,0:T(8,128)(2,1)} %bitcast.140), channel_id=1, source_target_pairs={{0,4},{4,0},{8,12},{12,8},{16,20},{20,16},{24,28},{28,24},{1,5},{5... | collective-permute-start | bytes 3538952 | tf_op jit(solution)/shard_map/ppermute | solution.py:388
  116.0 48.1 %collective-permute-start.35 = (bf16[4,128,1152]{2,1,0:T(8,128)(2,1)S(1)}, bf16[4,128,1152]{2,1,0:T(8,128)(2,1)S(1)}, u32[]{:S(2)}, u32[]{:S(2)}) collective-permute-start(bf16[4,128,1152]{2,1,0:T(8,128)(2,1)S(1)} %dynamic-slice_bitcast_fusion), channel_id=1, source_target_pairs={{0,4},{4,0},{8,12},{12,8},{16,20},{20,16},{24,28},{28,24},{1,5},{5... | collective-permute-start | bytes 3538952 | tf_op jit(solution)/shard_map/ppermute | solution.py:388
  124.2 14.8 %collective-permute-start.11 = (bf16[256,1024]{1,0:T(8,128)(2,1)S(1)}, bf16[256,1024]{1,0:T(8,128)(2,1)S(1)}, u32[]{:S(2)}, u32[]{:S(2)}) collective-permute-start(bf16[256,1024]{1,0:T(8,128)(2,1)S(1)} %add_convert_fusion.6), channel_id=1, source_target_pairs={{0,2},{1,3},{2,0},{3,1},{4,6},{5,7},{6,4},{7,5},{8,10},{9,11},{10,... | collective-permute-start | bytes 1572872 | tf_op jit(solution)/shard_map/ppermute | solution.py:388
  126.7 23.2 %collective-permute-start.14 = (bf16[256,1024]{1,0:T(8,128)(2,1)S(1)}, bf16[256,1024]{1,0:T(8,128)(2,1)S(1)}, u32[]{:S(2)}, u32[]{:S(2)}) collective-permute-start(bf16[256,1024]{1,0:T(8,128)(2,1)S(1)} %add_convert_fusion.4), channel_id=1, source_target_pairs={{0,2},{1,3},{2,0},{3,1},{4,6},{5,7},{6,4},{7,5},{8,10},{9,11},{10,... | collective-permute-start | bytes 1572872 | tf_op jit(solution)/shard_map/ppermute | solution.py:388
  127.4 61.3 %collective-permute-start.31 = (bf16[4,128,1152]{2,1,0:T(8,128)(2,1)S(1)}, bf16[4,128,1152]{2,1,0:T(8,128)(2,1)S(1)}, u32[]{:S(2)}, u32[]{:S(2)}) collective-permute-start(bf16[4,128,1152]{2,1,0:T(8,128)(2,1)S(1)} %dynamic-slice_bitcast_fusion.1), channel_id=1, source_target_pairs={{0,4},{4,0},{8,12},{12,8},{16,20},{20,16},{24,28},{28,24},{1,5},{5... | collective-permute-start | bytes 3538952 | tf_op jit(solution)/shard_map/ppermute | solution.py:388
  139.2 99.5 %collective-permute-start.12 = (bf16[256,1024]{1,0:T(8,128)(2,1)S(1)}, bf16[256,1024]{1,0:T(8,128)(2,1)S(1)}, u32[]{:S(2)}, u32[]{:S(2)}) collective-permute-start(bf16[256,1024]{1,0:T(8,128)(2,1)S(1)} %add_convert_fusion.5), channel_id=1, source_target_pairs={{0,1},{1,0},{2,3},{3,2},{4,5},{5,4},{6,7},{7,6},{8,9},{9,8},{10,11... | collective-permute-start | bytes 1572872 | tf_op jit(solution)/shard_map/ppermute | solution.py:388
  150.1 126.3 %collective-permute-start.15 = (bf16[256,1024]{1,0:T(8,128)(2,1)S(1)}, bf16[256,1024]{1,0:T(8,128)(2,1)}, u32[]{:S(2)}, u32[]{:S(2)}) collective-permute-start(bf16[256,1024]{1,0:T(8,128)(2,1)S(1)} %add_convert_fusion.3), channel_id=1, source_target_pairs={{0,1},{1,0},{2,3},{3,2},{4,5},{5,4},{6,7},{7,6},{8,9},{9,8},{10,11... | collective-permute-start | bytes 1572872 | tf_op jit(solution)/shard_map/ppermute | solution.py:388
  152.0 42.0 %collective-permute-start.40 = (bf16[128,1152]{0,1:T(8,128)(2,1)S(1)}, bf16[128,1152]{0,1:T(8,128)(2,1)S(1)}, u32[]{:S(2)}, u32[]{:S(2)}) collective-permute-start(bf16[128,1152]{0,1:T(8,128)(2,1)S(1)} %get-tuple-element.68), channel_id=1, source_target_pairs={{0,24},{4,28},{8,0},{12,4},{16,8},{20,12},{24,16},{28,20},{1,25},{... | collective-permute-start | bytes 884744 | tf_op jit(solution)/shard_map/ppermute | solution.py:393
  164.1 30.0 %collective-permute-start.41 = (bf16[128,1152]{0,1:T(8,128)(2,1)S(1)}, bf16[128,1152]{0,1:T(8,128)(2,1)S(1)}, u32[]{:S(2)}, u32[]{:S(2)}) collective-permute-start(bf16[128,1152]{0,1:T(8,128)(2,1)S(1)} %get-tuple-element.70), channel_id=1, source_target_pairs={{0,16},{4,20},{8,24},{12,28},{16,0},{20,4},{24,8},{28,12},{1,17},{... | collective-permute-start | bytes 884744 | tf_op jit(solution)/shard_map/ppermute | solution.py:393
  194.1 31.8 %collective-permute-start.37 = (bf16[128,1152]{1,0:T(8,128)(2,1)S(1)}, bf16[128,1152]{1,0:T(8,128)(2,1)S(1)}, u32[]{:S(2)}, u32[]{:S(2)}) collective-permute-start(bf16[128,1152]{1,0:T(8,128)(2,1)S(1)} %get-tuple-element.73), channel_id=1, source_target_pairs={{0,16},{4,20},{8,24},{12,28},{16,0},{20,4},{24,8},{28,12},{1,17},{... | collective-permute-start | bytes 884744 | tf_op jit(solution)/shard_map/ppermute | solution.py:393
  200.5 25.4 %collective-permute-start.38 = (bf16[128,1152]{1,0:T(8,128)(2,1)S(1)}, bf16[128,1152]{1,0:T(8,128)(2,1)S(1)}, u32[]{:S(2)}, u32[]{:S(2)}) collective-permute-start(bf16[128,1152]{1,0:T(8,128)(2,1)S(1)} %get-tuple-element.72), channel_id=1, source_target_pairs={{0,8},{4,12},{8,16},{12,20},{16,24},{20,28},{24,0},{28,4},{1,9},{5... | collective-permute-start | bytes 884744 | tf_op jit(solution)/shard_map/ppermute | solution.py:393
  206.2 66.8 %collective-permute-start.32 = (bf16[128,1152]{1,0:T(8,128)(2,1)}, bf16[128,1152]{1,0:T(8,128)(2,1)}, u32[]{:S(2)}, u32[]{:S(2)}) collective-permute-start(bf16[128,1152]{1,0:T(8,128)(2,1)} %get-tuple-element.74), channel_id=1, source_target_pairs={{0,24},{4,28},{8,0},{12,4},{16,8},{20,12},{24,16},{28,20},{1,25},{... | collective-permute-start | bytes 884744 | tf_op jit(solution)/shard_map/ppermute | solution.py:393
  225.9 47.1 %collective-permute-start.33 = (bf16[128,1152]{1,0:T(8,128)(2,1)}, bf16[128,1152]{1,0:T(8,128)(2,1)}, u32[]{:S(2)}, u32[]{:S(2)}) collective-permute-start(bf16[128,1152]{1,0:T(8,128)(2,1)} %get-tuple-element.76), channel_id=1, source_target_pairs={{0,16},{4,20},{8,24},{12,28},{16,0},{20,4},{24,8},{28,12},{1,17},{... | collective-permute-start | bytes 884744 | tf_op jit(solution)/shard_map/ppermute | solution.py:393
  225.9 47.1 %collective-permute-start.34 = (bf16[128,1152]{1,0:T(8,128)(2,1)}, bf16[128,1152]{1,0:T(8,128)(2,1)}, u32[]{:S(2)}, u32[]{:S(2)}) collective-permute-start(bf16[128,1152]{1,0:T(8,128)(2,1)} %get-tuple-element.75), channel_id=1, source_target_pairs={{0,8},{4,12},{8,16},{12,20},{16,24},{20,28},{24,0},{28,4},{1,9},{5... | collective-permute-start | bytes 884744 | tf_op jit(solution)/shard_map/ppermute | solution.py:393
  258.9 34.1 %collective-permute-start.16 = (bf16[4,512,256]{2,1,0:T(8,128)(2,1)}, bf16[4,512,256]{2,1,0:T(8,128)(2,1)S(1)}, u32[]{:S(2)}, u32[]{:S(2)}) collective-permute-start(bf16[4,512,256]{2,1,0:T(8,128)(2,1)} %get-tuple-element.39), channel_id=1, source_target_pairs={{0,4},{4,0},{8,12},{12,8},{16,20},{20,16},{24,28},{28,24},{1,5},{5... | collective-permute-start | bytes 3145736 | tf_op jit(solution)/shard_map/ppermute | solution.py:388
  294.3 23.3 %collective-permute-start.18 = (bf16[512,256]{1,0:T(8,128)(2,1)}, bf16[512,256]{1,0:T(8,128)(2,1)}, u32[]{:S(2)}, u32[]{:S(2)}) collective-permute-start(bf16[512,256]{1,0:T(8,128)(2,1)} %get-tuple-element.78), channel_id=1, source_target_pairs={{0,16},{4,20},{8,24},{12,28},{16,0},{20,4},{24,8},{28,12},{1,17},{... | collective-permute-start | bytes 786440 | tf_op jit(solution)/shard_map/ppermute | solution.py:393
  298.2 19.4 %collective-permute-start.19 = (bf16[512,256]{1,0:T(8,128)(2,1)}, bf16[512,256]{1,0:T(8,128)(2,1)}, u32[]{:S(2)}, u32[]{:S(2)}) collective-permute-start(bf16[512,256]{1,0:T(8,128)(2,1)} %get-tuple-element.77), channel_id=1, source_target_pairs={{0,8},{4,12},{8,16},{12,20},{16,24},{20,28},{24,0},{28,4},{1,9},{5... | collective-permute-start | bytes 786440 | tf_op jit(solution)/shard_map/ppermute | solution.py:393
  301.2 28.7 %collective-permute-start.27 = (bf16[4,128,256]{1,2,0:T(8,128)(2,1)}, bf16[4,128,256]{1,2,0:T(8,128)(2,1)}, u32[]{:S(2)}, u32[]{:S(2)}) collective-permute-start(bf16[4,128,256]{1,2,0:T(8,128)(2,1)} %bitcast.143), channel_id=1, source_target_pairs={{0,4},{4,0},{8,12},{12,8},{16,20},{20,16},{24,28},{28,24},{1,5},{5... | collective-permute-start | bytes 786440 | tf_op jit(solution)/shard_map/ppermute | solution.py:388
  326.6 13.9 %collective-permute-start.23 = (bf16[4,128,512]{2,1,0:T(8,128)(2,1)S(1)}, bf16[4,128,512]{2,1,0:T(8,128)(2,1)S(1)}, u32[]{:S(2)}, u32[]{:S(2)}) collective-permute-start(bf16[4,128,512]{2,1,0:T(8,128)(2,1)S(1)} %dynamic-slice_bitcast_fusion.2), channel_id=1, source_target_pairs={{0,4},{4,0},{8,12},{12,8},{16,20},{20,16},{24,28},{28,24},{1,5},{5... | collective-permute-start | bytes 1572872 | tf_op jit(solution)/shard_map/ppermute | solution.py:388
  (72 other events, 640.7 us)
